TPU v7x, 32 devices: a whole 2x2x4 slice. The times are simulated.
32 devices in a mesh: segment: 2 (over x), tensor: 16 (over z, y, core).
Axes of the slice: x: 2, y: 2, z: 4, core: 2. Of those that a mesh axis runs over, the one named last changes fastest.
Arguments:
- step_inputs: bfloat16 [3, 16, 8192], P(None, None, 'tensor'), may hold values from -6 to 6
- norm_gain: float32 [2, 8192], P('segment'), may hold values from 0.1 to 1.9
- query_weight: bfloat16 [2, 8192, 8192], P('segment', None, 'tensor'), may hold values from -0.0625 to 0.0625
- kv_weight: bfloat16 [2, 8192, 2, 1024], P('segment', None, None, 'tensor'), may hold values from -0.125 to 0.125
- out_weight: bfloat16 [2, 8192, 8192], P('segment', None, 'tensor'), may hold values from -0.125 to 0.125
- kv_cache: bfloat16 [2, 16, 3, 128, 256], P('segment', 'tensor'), as said below
- block_table: int32 [16, 2], replicated, may hold values from 0 to 2, as said below
- prefix_len: int32 [16], replicated, may hold values from 1 to 256, as said below
- parents: int32 [3, 16], replicated, may hold values from 0 to 15
Outputs:
- received: bfloat16 [2, 3, 16, 8192], P('segment', None, None, 'tensor')
Inputs may be any that keep to these rules, and one draw needn't show every extreme that they name: `block_table`: every row of one source has the same first entry; its second entry is one of two blocks of that source, each of them used by some row; no block serves two sources. `prefix_len`: some row holds 256 tokens. `kv_cache`: copies c and c' are equal when c * 64 // (number of copies) // 8 equals the same for c'.
All inputs are finite; a program needn't handle non-finite values.
Results may differ from a plain program's by a relative error of at most 0.012.
The roundings to bfloat16 on the way count: a program that leaves them out, or rounds other values in their place, can miss the bound.
Values may be sent and summed in bfloat16 or wider, within the bound.
A program may use at most 64 MiB of HBM per device.

v0:
```python
import jax
import jax.numpy as jnp
from jax import lax
from jax.sharding import PartitionSpec as P

KV_HEADS = 8
HEAD_SIZE = 128
BEAMS = 16
BLOCK = 128
STEPS = 3
SOURCES = 1
GROUP = 8


ROPE_BASE = 1000000.0
NORM_EPS = 1e-06
MASK_FLOOR = -1e30


def shifted(block, axis, distance):
    devices = range(lax.axis_size(axis))
    route = [((i - distance) % len(devices), i) for i in devices]
    return lax.ppermute(block, axis, route)


def normalize(rows_in, gain):
    widened = rows_in.astype(jnp.float32)
    mean_square = jnp.mean(widened * widened, axis=-1, keepdims=True)
    return (widened * lax.rsqrt(mean_square + NORM_EPS) * gain).astype(jnp.bfloat16)


def rotate(values, positions):
    half_size = values.shape[-1] // 2
    exponent = jnp.arange(half_size, dtype=jnp.float32) * (2.0 / values.shape[-1])
    frequency = jnp.power(jnp.float32(ROPE_BASE), -exponent)
    angles = positions.astype(jnp.float32)[:, None] * frequency[None, :]
    angles = jnp.concatenate([angles, angles], axis=-1)[:, None, :]
    front_part = values[..., :half_size]
    back_part = values[..., half_size:]
    turned = jnp.concatenate([-back_part, front_part], axis=-1)
    return values * jnp.cos(angles) + turned * jnp.sin(angles)


def ancestry(parents):
    rows_all = parents.shape[1]
    source_start = jnp.arange(rows_all, dtype=jnp.int32) // BEAMS * BEAMS
    lineage = []
    root_table = []
    for later_step in range(STEPS):
        current = jnp.arange(rows_all, dtype=jnp.int32)
        lineage_list = [current]
        for earlier in range(later_step, 0, -1):
            current = source_start + parents[earlier][current]
            lineage_list.append(current)
        lineage_list = lineage_list[::-1] + [current] * (STEPS - later_step - 1)
        lineage.append(jnp.stack(lineage_list))
        root_table.append(source_start + parents[0][current])
    return (jnp.stack(lineage), jnp.stack(root_table))


def per_device(
    step_inputs,
    norm_gain,
    query_weight,
    kv_weight,
    out_weight,
    kv_cache,
    block_table,
    prefix_len,
    parents,
):
    segments = lax.axis_size("segment")
    segment_id = lax.axis_index("segment")
    device_id = lax.axis_index("tensor")
    local_width = step_inputs.shape[2]
    rows_all = step_inputs.shape[1]
    head_count = query_weight.shape[2] // HEAD_SIZE
    kv_owner = device_id * head_count // GROUP
    score_scale = HEAD_SIZE ** (-0.5)
    lineage, root_table = ancestry(parents)
    gain = norm_gain[0]
    query_local = query_weight[0]
    kv_local = kv_weight[0]
    out_local = out_weight[0]
    cache_local = kv_cache[0, 0]

    def project_rows(piece):
        return jnp.dot(piece, out_local, preferred_element_type=jnp.float32)

    def advance(loop_state, tick_index, item_base, item_count):
        incoming, history, received = loop_state
        local_item = tick_index - segment_id
        active = (local_item >= 0) & (local_item < item_count)
        item_index = item_base + jnp.clip(local_item, 0, item_count - 1)
        step_index = item_index // SOURCES
        source = item_index % SOURCES
        row_start = source * BEAMS
        fresh_rows = lax.dynamic_slice(
            step_inputs, (step_index, row_start, 0), (1, BEAMS, local_width)
        )[0]
        current = jnp.where(segment_id == 0, fresh_rows, incoming)
        full_rows = lax.all_gather(current, "tensor", axis=1, tiled=True)
        normed = normalize(full_rows, gain)
        queries = jnp.dot(normed, query_local, preferred_element_type=jnp.float32).reshape(
            BEAMS, head_count, HEAD_SIZE
        )
        partial_kv = jnp.einsum(
            "rd,dkc->rkc", normed, kv_local, preferred_element_type=jnp.float32
        ).astype(jnp.bfloat16)
        gathered_kv = lax.all_gather(partial_kv, "tensor", axis=2, tiled=True)
        gathered_kv = gathered_kv.reshape(BEAMS, 2, HEAD_SIZE, KV_HEADS)
        own_kv = lax.dynamic_slice_in_dim(gathered_kv, kv_owner, 1, 3)[..., 0]
        lineage_rows = lax.dynamic_slice(lineage, (step_index, 0, row_start), (1, STEPS, BEAMS))[0]
        root_rows = lax.dynamic_slice(root_table, (step_index, row_start), (1, BEAMS))[0]
        lengths = prefix_len[root_rows]
        positions = lengths + step_index
        new_key = rotate(own_kv[:, 0:1].astype(jnp.float32), positions).astype(jnp.bfloat16)[:, 0]
        turned_query = rotate(queries, positions).astype(jnp.bfloat16)
        new_entry = jnp.stack([new_key, own_kv[:, 1]], axis=1)
        updated = lax.dynamic_update_slice(history, new_entry[None], (step_index, row_start, 0, 0))
        history = jnp.where(active, updated, history)
        past = history[jnp.arange(STEPS, dtype=jnp.int32)[:, None], lineage_rows]
        history_mask = jnp.arange(STEPS, dtype=jnp.int32) <= step_index
        prefix_mask = jnp.arange(2 * BLOCK, dtype=jnp.int32)[None, :] < lengths[:, None]
        table_rows = block_table[root_rows]
        blocks = cache_local[table_rows].reshape(BEAMS, 2 * BLOCK, 2 * HEAD_SIZE)
        prefix_scores = jnp.einsum(
            "rhd,rkd->rhk",
            turned_query,
            blocks[:, :, :HEAD_SIZE],
            preferred_element_type=jnp.float32,
        )
        prefix_scores = jnp.where(prefix_mask[:, None, :], prefix_scores * score_scale, MASK_FLOOR)
        history_scores = (
            jnp.einsum(
                "rhd,trd->rht", turned_query, past[:, :, 0], preferred_element_type=jnp.float32
            )
            * score_scale
        )
        history_scores = jnp.where(history_mask[None, None, :], history_scores, MASK_FLOOR)
        highest = jnp.maximum(jnp.max(prefix_scores, axis=-1), jnp.max(history_scores, axis=-1))[
            ..., None
        ]
        prefix_exp = jnp.exp(prefix_scores - highest)
        history_exp = jnp.exp(history_scores - highest)
        denominator = jnp.sum(prefix_exp, axis=-1, keepdims=True) + jnp.sum(
            history_exp, axis=-1, keepdims=True
        )
        prefix_probs = (prefix_exp / denominator).astype(jnp.bfloat16)
        history_probs = (history_exp / denominator).astype(jnp.bfloat16)
        mixture = jnp.einsum(
            "rhk,rkd->rhd",
            prefix_probs,
            blocks[:, :, HEAD_SIZE:],
            preferred_element_type=jnp.float32,
        )
        mixture = mixture + jnp.einsum(
            "rht,trd->rhd", history_probs, past[:, :, 1], preferred_element_type=jnp.float32
        )
        attended = mixture.reshape(BEAMS, head_count * HEAD_SIZE).astype(jnp.bfloat16)
        update = project_rows(lax.all_gather(attended, "tensor", axis=1, tiled=True))
        result = (current.astype(jnp.float32) + update).astype(jnp.bfloat16)
        passed = shifted(result, "segment", 1)
        sender = (segment_id + segments - 1) % segments
        sent_local = tick_index - sender
        sent_valid = (sent_local >= 0) & (sent_local < item_count)
        sent_item = item_base + jnp.clip(sent_local, 0, item_count - 1)
        sent_step = sent_item // SOURCES
        sent_row = sent_item % SOURCES * BEAMS
        stored = lax.dynamic_update_slice(received, passed[None], (sent_step, sent_row, 0))
        received = jnp.where(sent_valid, stored, received)
        return (passed, history, received)

    loop_state = (
        jnp.zeros((BEAMS, local_width), jnp.bfloat16),
        jnp.zeros((STEPS, rows_all, 2, HEAD_SIZE), jnp.bfloat16),
        jnp.zeros((STEPS, rows_all, local_width), jnp.bfloat16),
    )
    sweep_loop_state = loop_state
    item_count = STEPS * SOURCES

    def scan_step(state_in, tick_index):
        return (advance(state_in, tick_index, 0, item_count), None)

    ticks = jnp.arange(item_count + segments - 1, dtype=jnp.int32)
    sweep_loop_state, unused = lax.scan(scan_step, sweep_loop_state, ticks)
    loop_state = sweep_loop_state
    return loop_state[2][None]


def solution(mesh):
    return jax.shard_map(
        per_device,
        mesh=mesh,
        in_specs=(
            P(None, None, "tensor"),
            P("segment", None),
            P("segment", None, "tensor"),
            P("segment", None, None, "tensor"),
            P("segment", None, "tensor"),
            P("segment", "tensor", None, None, None),
            P(),
            P(),
            P(),
        ),
        out_specs=P("segment", None, None, "tensor"),
        check_vma=False,
    )
```

profile of v0, /device:TPU:0, one launch (start us, length us, event | category | flops | bytes accessed | tf_op | source)
XLA Modules:
  0.0 343.2 jit_solution(172588675042118891)
XLA Ops:
  5.4 337.2 %while.17 = (s32[]{:T(128)}, bf16[16,512]{1,0:T(8,128)(2,1)S(1)}, bf16[3,16,2,128]{3,2,1,0:T(2,128)(2,1)S(1)}, bf16[3,16,512]{2,1,0:T(8,128)(2,1)S(1)}, pred[]{:...) while((s32[]{:T(128)}, bf16[16,512]{1,0:T(8,128)(2,1)S(1)}, ...), condition=%wide.region_6.7_spmd, body=%wide.region_0.6_spmd.sunk | while | flops 312203328 | bytes 28216092 | solution.py:186
  8.1 23.8 %all_gather.24 = bf16[16,8192]{1,0:T(8,128)(2,1)S(1)} all-gather(bf16[16,512]{1,0:T(8,128)(2,1)S(1)} %bitcast_select_fusion.3), channel_id=1, replica_groups=mesh['segment'=2,'tensor'=16] {'tensor'}, dimensions={1}, use_global_device_ids=true | all-gather | bytes 278528 | tf_op jit(solution)/shard_map/while/body/eval_jaxpr/all_gather | solution.py:102
  32.1 0.9 convolution_convert_fusion.2
  33.2 18.9 %all_gather.25 = bf16[16,2,1024]{0,1,2:T(2,128)(2,1)S(1)} all-gather(bf16[16,2,64]{0,1,2:T(2,128)(2,1)S(1)} %copy.77), channel_id=1, replica_groups=mesh['segment'=2,'tensor'=16] {'tensor'}, dimensions={2}, use_global_device_ids=true | all-gather | bytes 69632 | tf_op jit(solution)/shard_map/while/body/eval_jaxpr/all_gather | solution.py:110
  53.2 0.9 gather_fusion.3
  54.1 4.6 %fusion.83 = f32[16,512]{1,0:T(8,128)S(1)} fusion(bf16[8192,512]{1,0:T(8,128)(2,1)} %get-tuple-element.631, bf16[16,8192]{1,0:T(8,128)(2,1)S(1)} %all_gather.24, f32[8192]{0:T(1024)S(1)} %bitcast.161, f32[16]{0:T(128)S(1)} %add_rsqrt_fusion.2), kind=kOutput, calls=%fused_computation.31.clone.1 | convolution fusion | flops 134742016 | bytes 8716352 | tf_op jit(solution)/shard_map/while/body/eval_jaxpr/dot_general | solution.py:104
  59.7 2.0 gather_fusion.1
  62.0 1.7 fusion.86
  63.9 1.5 fusion.94
  65.7 19.5 %all_gather.26 = bf16[16,8192]{1,0:T(8,128)(2,1)S(1)} all-gather(bf16[16,512]{1,0:T(8,128)(2,1)S(1)} %bitcast.164), channel_id=1, replica_groups=mesh['segment'=2,'tensor'=16] {'tensor'}, dimensions={1}, use_global_device_ids=true | all-gather | bytes 278528 | tf_op jit(solution)/shard_map/while/body/eval_jaxpr/all_gather | solution.py:161
  85.2 4.6 %fusion.96 = bf16[16,512]{1,0:T(8,128)(2,1)S(1)} fusion(bf16[16,8192]{1,0:T(8,128)(2,1)S(1)} %all_gather.26, bf16[8192,512]{1,0:T(8,128)(2,1)} %get-tuple-element.637, bf16[16,512]{1,0:T(8,128)(2,1)S(1)} %bitcast_select_fusion.3), kind=kOutput, calls=%fused_computation.17.clone.1 | convolution fusion | flops 134242304 | bytes 8683520 | tf_op jit(solution)/shard_map/while/body/eval_jaxpr/dot_general | solution.py:88
  89.8 1.5 collective-permute-start
  91.9 1.6 collective-permute-done
  96.3 18.2 %all_gather.24 = bf16[16,8192]{1,0:T(8,128)(2,1)S(1)} all-gather(bf16[16,512]{1,0:T(8,128)(2,1)S(1)} %bitcast_select_fusion.3), channel_id=1, replica_groups=mesh['segment'=2,'tensor'=16] {'tensor'}, dimensions={1}, use_global_device_ids=true | all-gather | bytes 278528 | tf_op jit(solution)/shard_map/while/body/eval_jaxpr/all_gather | solution.py:102
  114.7 0.9 convolution_convert_fusion.2
  115.8 20.3 %all_gather.25 = bf16[16,2,1024]{0,1,2:T(2,128)(2,1)S(1)} all-gather(bf16[16,2,64]{0,1,2:T(2,128)(2,1)S(1)} %copy.77), channel_id=1, replica_groups=mesh['segment'=2,'tensor'=16] {'tensor'}, dimensions={2}, use_global_device_ids=true | all-gather | bytes 69632 | tf_op jit(solution)/shard_map/while/body/eval_jaxpr/all_gather | solution.py:110
  138.1 4.6 %fusion.83 = f32[16,512]{1,0:T(8,128)S(1)} fusion(bf16[8192,512]{1,0:T(8,128)(2,1)} %get-tuple-element.631, bf16[16,8192]{1,0:T(8,128)(2,1)S(1)} %all_gather.24, f32[8192]{0:T(1024)S(1)} %bitcast.161, f32[16]{0:T(128)S(1)} %add_rsqrt_fusion.2), kind=kOutput, calls=%fused_computation.31.clone.1 | convolution fusion | flops 134742016 | bytes 8716352 | tf_op jit(solution)/shard_map/while/body/eval_jaxpr/dot_general | solution.py:104
  143.7 2.0 gather_fusion.1
  146.0 1.7 fusion.86
  147.9 1.5 fusion.94
  149.7 18.2 %all_gather.26 = bf16[16,8192]{1,0:T(8,128)(2,1)S(1)} all-gather(bf16[16,512]{1,0:T(8,128)(2,1)S(1)} %bitcast.164), channel_id=1, replica_groups=mesh['segment'=2,'tensor'=16] {'tensor'}, dimensions={1}, use_global_device_ids=true | all-gather | bytes 278528 | tf_op jit(solution)/shard_map/while/body/eval_jaxpr/all_gather | solution.py:161
  167.8 4.6 %fusion.96 = bf16[16,512]{1,0:T(8,128)(2,1)S(1)} fusion(bf16[16,8192]{1,0:T(8,128)(2,1)S(1)} %all_gather.26, bf16[8192,512]{1,0:T(8,128)(2,1)} %get-tuple-element.637, bf16[16,512]{1,0:T(8,128)(2,1)S(1)} %bitcast_select_fusion.3), kind=kOutput, calls=%fused_computation.17.clone.1 | convolution fusion | flops 134242304 | bytes 8683520 | tf_op jit(solution)/shard_map/while/body/eval_jaxpr/dot_general | solution.py:88
  172.4 1.5 collective-permute-start
  174.5 1.6 collective-permute-done
  178.9 19.5 %all_gather.24 = bf16[16,8192]{1,0:T(8,128)(2,1)S(1)} all-gather(bf16[16,512]{1,0:T(8,128)(2,1)S(1)} %bitcast_select_fusion.3), channel_id=1, replica_groups=mesh['segment'=2,'tensor'=16] {'tensor'}, dimensions={1}, use_global_device_ids=true | all-gather | bytes 278528 | tf_op jit(solution)/shard_map/while/body/eval_jaxpr/all_gather | solution.py:102
  198.6 0.9 convolution_convert_fusion.2
  199.6 18.9 %all_gather.25 = bf16[16,2,1024]{0,1,2:T(2,128)(2,1)S(1)} all-gather(bf16[16,2,64]{0,1,2:T(2,128)(2,1)S(1)} %copy.77), channel_id=1, replica_groups=mesh['segment'=2,'tensor'=16] {'tensor'}, dimensions={2}, use_global_device_ids=true | all-gather | bytes 69632 | tf_op jit(solution)/shard_map/while/body/eval_jaxpr/all_gather | solution.py:110
  219.7 0.9 gather_fusion.3
  220.6 4.6 %fusion.83 = f32[16,512]{1,0:T(8,128)S(1)} fusion(bf16[8192,512]{1,0:T(8,128)(2,1)} %get-tuple-element.631, bf16[16,8192]{1,0:T(8,128)(2,1)S(1)} %all_gather.24, f32[8192]{0:T(1024)S(1)} %bitcast.161, f32[16]{0:T(128)S(1)} %add_rsqrt_fusion.2), kind=kOutput, calls=%fused_computation.31.clone.1 | convolution fusion | flops 134742016 | bytes 8716352 | tf_op jit(solution)/shard_map/while/body/eval_jaxpr/dot_general | solution.py:104
  226.2 2.0 gather_fusion.1
  228.4 1.7 fusion.86
  230.4 1.5 fusion.94
  232.1 19.5 %all_gather.26 = bf16[16,8192]{1,0:T(8,128)(2,1)S(1)} all-gather(bf16[16,512]{1,0:T(8,128)(2,1)S(1)} %bitcast.164), channel_id=1, replica_groups=mesh['segment'=2,'tensor'=16] {'tensor'}, dimensions={1}, use_global_device_ids=true | all-gather | bytes 278528 | tf_op jit(solution)/shard_map/while/body/eval_jaxpr/all_gather | solution.py:161
  251.6 4.6 %fusion.96 = bf16[16,512]{1,0:T(8,128)(2,1)S(1)} fusion(bf16[16,8192]{1,0:T(8,128)(2,1)S(1)} %all_gather.26, bf16[8192,512]{1,0:T(8,128)(2,1)} %get-tuple-element.637, bf16[16,512]{1,0:T(8,128)(2,1)S(1)} %bitcast_select_fusion.3), kind=kOutput, calls=%fused_computation.17.clone.1 | convolution fusion | flops 134242304 | bytes 8683520 | tf_op jit(solution)/shard_map/while/body/eval_jaxpr/dot_general | solution.py:88
  256.2 1.5 collective-permute-start
  258.3 1.6 collective-permute-done
  262.7 18.2 %all_gather.24 = bf16[16,8192]{1,0:T(8,128)(2,1)S(1)} all-gather(bf16[16,512]{1,0:T(8,128)(2,1)S(1)} %bitcast_select_fusion.3), channel_id=1, replica_groups=mesh['segment'=2,'tensor'=16] {'tensor'}, dimensions={1}, use_global_device_ids=true | all-gather | bytes 278528 | tf_op jit(solution)/shard_map/while/body/eval_jaxpr/all_gather | solution.py:102
  281.1 0.9 convolution_convert_fusion.2
  282.2 20.3 %all_gather.25 = bf16[16,2,1024]{0,1,2:T(2,128)(2,1)S(1)} all-gather(bf16[16,2,64]{0,1,2:T(2,128)(2,1)S(1)} %copy.77), channel_id=1, replica_groups=mesh['segment'=2,'tensor'=16] {'tensor'}, dimensions={2}, use_global_device_ids=true | all-gather | bytes 69632 | tf_op jit(solution)/shard_map/while/body/eval_jaxpr/all_gather | solution.py:110
  303.6 0.9 gather_fusion.3
  304.5 4.6 %fusion.83 = f32[16,512]{1,0:T(8,128)S(1)} fusion(bf16[8192,512]{1,0:T(8,128)(2,1)} %get-tuple-element.631, bf16[16,8192]{1,0:T(8,128)(2,1)S(1)} %all_gather.24, f32[8192]{0:T(1024)S(1)} %bitcast.161, f32[16]{0:T(128)S(1)} %add_rsqrt_fusion.2), kind=kOutput, calls=%fused_computation.31.clone.1 | convolution fusion | flops 134742016 | bytes 8716352 | tf_op jit(solution)/shard_map/while/body/eval_jaxpr/dot_general | solution.py:104
  310.1 2.0 gather_fusion.1
  312.3 1.7 fusion.86
  314.3 1.5 fusion.94
  316.0 18.2 %all_gather.26 = bf16[16,8192]{1,0:T(8,128)(2,1)S(1)} all-gather(bf16[16,512]{1,0:T(8,128)(2,1)S(1)} %bitcast.164), channel_id=1, replica_groups=mesh['segment'=2,'tensor'=16] {'tensor'}, dimensions={1}, use_global_device_ids=true | all-gather | bytes 278528 | tf_op jit(solution)/shard_map/while/body/eval_jaxpr/all_gather | solution.py:161
  334.2 4.6 %fusion.96 = bf16[16,512]{1,0:T(8,128)(2,1)S(1)} fusion(bf16[16,8192]{1,0:T(8,128)(2,1)S(1)} %all_gather.26, bf16[8192,512]{1,0:T(8,128)(2,1)} %get-tuple-element.637, bf16[16,512]{1,0:T(8,128)(2,1)S(1)} %bitcast_select_fusion.3), kind=kOutput, calls=%fused_computation.17.clone.1 | convolution fusion | flops 134242304 | bytes 8683520 | tf_op jit(solution)/shard_map/while/body/eval_jaxpr/dot_general | solution.py:88
  338.8 1.5 collective-permute-start
  340.9 1.6 collective-permute-done
  (221 shorter events, 27.3 us)
Async XLA Ops:
  0.0 5.2 %copy-start.5 = (s32[16,2]{0,1:T(2,128)S(1)}, s32[16,2]{0,1:T(2,128)}, u32[]{:S(2)}) copy-start(s32[16,2]{0,1:T(2,128)} %param.17) | copy-start | bytes 388
  0.0 5.3 %copy-start.1 = (bf16[1,1,3,128,256]{4,3,2,1,0:T(8,128)(2,1)S(1)}, bf16[1,1,3,128,256]{4,3,2,1,0:T(8,128)(2,1)}, u32[]{:S(2)}) copy-start(bf16[1,1,3,128,256]{4,3,2,1,0:T(8,128)(2,1)} %param.16) | copy-start | bytes 589828
  0.0 5.3 %copy-start.2 = (bf16[1,8192,2,64]{1,3,2,0:T(8,128)(2,1)S(1)}, bf16[1,8192,2,64]{1,3,2,0:T(8,128)(2,1)}, u32[]{:S(2)}) copy-start(bf16[1,8192,2,64]{1,3,2,0:T(8,128)(2,1)} %param.14) | copy-start | bytes 6291460
  0.0 5.3 %copy-start.3 = (f32[1,8192]{1,0:T(1,128)S(1)}, f32[1,8192]{1,0:T(1,128)}, u32[]{:S(2)}) copy-start(f32[1,8192]{1,0:T(1,128)} %param.12) | copy-start | bytes 98308
  0.0 5.3 %copy-start = (s32[16]{0:T(128)S(1)}, s32[16]{0:T(128)}, u32[]{:S(2)}) copy-start(s32[16]{0:T(128)} %param.18) | copy-start | bytes 196
  89.8 3.8 %collective-permute-start = (bf16[16,512]{1,0:T(8,128)(2,1)S(1)}, bf16[16,512]{1,0:T(8,128)(2,1)S(1)}, u32[]{:S(2)}, u32[]{:S(2)}) collective-permute-start(bf16[16,512]{1,0:T(8,128)(2,1)S(1)} %fusion.96), channel_id=1, source_target_pairs={{16,0},{0,16},{17,1},{1,17},{18,2},{2,18},{19,3},{3,19},{20,4},{4,... | collective-permute-start | bytes 49160 | tf_op jit(solution)/shard_map/while/body/eval_jaxpr/ppermute | solution.py:23
  172.4 3.8 %collective-permute-start = (bf16[16,512]{1,0:T(8,128)(2,1)S(1)}, bf16[16,512]{1,0:T(8,128)(2,1)S(1)}, u32[]{:S(2)}, u32[]{:S(2)}) collective-permute-start(bf16[16,512]{1,0:T(8,128)(2,1)S(1)} %fusion.96), channel_id=1, source_target_pairs={{16,0},{0,16},{17,1},{1,17},{18,2},{2,18},{19,3},{3,19},{20,4},{4,... | collective-permute-start | bytes 49160 | tf_op jit(solution)/shard_map/while/body/eval_jaxpr/ppermute | solution.py:23
  256.2 3.8 %collective-permute-start = (bf16[16,512]{1,0:T(8,128)(2,1)S(1)}, bf16[16,512]{1,0:T(8,128)(2,1)S(1)}, u32[]{:S(2)}, u32[]{:S(2)}) collective-permute-start(bf16[16,512]{1,0:T(8,128)(2,1)S(1)} %fusion.96), channel_id=1, source_target_pairs={{16,0},{0,16},{17,1},{1,17},{18,2},{2,18},{19,3},{3,19},{20,4},{4,... | collective-permute-start | bytes 49160 | tf_op jit(solution)/shard_map/while/body/eval_jaxpr/ppermute | solution.py:23
  338.8 3.8 %collective-permute-start = (bf16[16,512]{1,0:T(8,128)(2,1)S(1)}, bf16[16,512]{1,0:T(8,128)(2,1)S(1)}, u32[]{:S(2)}, u32[]{:S(2)}) collective-permute-start(bf16[16,512]{1,0:T(8,128)(2,1)S(1)} %fusion.96), channel_id=1, source_target_pairs={{16,0},{0,16},{17,1},{1,17},{18,2},{2,18},{19,3},{3,19},{20,4},{4,... | collective-permute-start | bytes 49160 | tf_op jit(solution)/shard_map/while/body/eval_jaxpr/ppermute | solution.py:23
  342.5 0.6 copy-start.4
where the time goes:
time: 344 us; the launch traced here: 343 us
  blocking collectives  233 us (68%)
  matrix products  54.9 us (16%)
  local copies, waits for them, and re-layouts  27.8 us (8%)
  other arithmetic  8.74 us (3%)
  waiting for transfers between devices  6.44 us (2%)
  starting transfers between devices  6.03 us (2%)
  loops' own time  5.8 us (2%)
    all_gather x4, blocking collectives, advance(): full_rows = lax.all_gather(current, 'tensor', axis=1, tiled=True)  79.6 us
    all_gather x4, blocking collectives, advance(): gathered_kv = lax.all_gather(partial_kv, 'tensor', axis=2, tiled=True)  78.3 us
    all_gather x4, blocking collectives, advance(): lax.all_gather(attended, 'tensor', axis=1, tiled=True)  75.3 us
    dot_general x4, matrix products, advance(): jnp.dot(normed, query_local, preferred_element_type=jnp.float32)  18.5 us
    dot_general x4, matrix products, project_rows(): return jnp.dot(piece, out_local, preferred_element_type=jnp.float32)  18.3 us
    gather x4, local copies, waits for them, and re-layouts, advance(): blocks = cache_local[table_rows].reshape(BEAMS, 2 * BLOCK, 2 * HEAD_SIZE)  8.11 us
  transfers between devices with their start and end apart: 4, of which 4 were waited for; matrix products, arithmetic and copies ran while one was open for 0% of the time, Pallas kernels for 0%

commit v1 on v0

v1 whole, which is shorter than its diff:
```python
import functools

import jax
import jax.numpy as jnp
from jax import lax
from jax.experimental import pallas as pl
from jax.experimental.pallas import tpu as pltpu
from jax.sharding import PartitionSpec as P

KV_HEADS = 8
HEAD_SIZE = 128
BEAMS = 16
BLOCK = 128
GROUP = 8
ROPE_BASE = 1000000.0
NORM_EPS = 1e-06
MASK_FLOOR = -1e30
MESH = pl.DeviceIdType.MESH
CORES = 2
COLUMNS = 2


def dot(a, b):
    return jnp.dot(a, b, preferred_element_type=jnp.float32)


def dot_nt(a, b):
    return lax.dot_general(a, b, (((1,), (1,)), ((), ())), preferred_element_type=jnp.float32)


class Gather:
    def __init__(self, buf, send, recv, me, lines):
        self.buf, self.send, self.recv, self.lines = buf, send, recv, lines
        self.me = me
        self.a = me // (COLUMNS * CORES)
        self.b = (me // CORES) % COLUMNS
        self.c = me % CORES
        self.started = []

    def slot(self, a, b, c):
        return (a * COLUMNS + b) * CORES + c

    def line(self, i):
        return lax.rem(self.a + i, self.lines)

    def peers(self):
        found = [self.slot(self.line(i), self.b, self.c) for i in range(1, self.lines)]
        return found + [self.across(), self.sibling()]

    def across(self):
        return self.slot(self.a, 1 - self.b, self.c)

    def sibling(self):
        return self.slot(self.a, self.b, 1 - self.c)

    def push(self, slot, target):
        copy = pltpu.make_async_remote_copy(
            src_ref=self.buf.at[slot],
            dst_ref=self.buf.at[slot],
            send_sem=self.send.at[len(self.started)],
            recv_sem=self.recv.at[slot],
            device_id={"tensor": target},
            device_id_type=MESH,
        )
        copy.start()
        self.started.append(copy)

    def arrived(self, slot):
        pltpu.make_async_remote_copy(
            src_ref=self.buf.at[slot],
            dst_ref=self.buf.at[slot],
            send_sem=self.send.at[0],
            recv_sem=self.recv.at[slot],
            device_id={"tensor": self.sibling()},
            device_id_type=MESH,
        ).wait_recv()

    def first(self, use):
        for peer in self.peers():
            self.push(self.me, peer)
        use(self.me)

    def second(self, use):
        for i in [1, self.lines - 1] + list(range(2, self.lines - 1)):
            slot = self.slot(self.line(i), self.b, self.c)
            self.arrived(slot)
            self.push(slot, self.across())
            self.push(slot, self.sibling())
            use(slot)

    def third(self, use):
        for i in [0, 1, self.lines - 1] + list(range(2, self.lines - 1)):
            slot = self.slot(self.line(i), 1 - self.b, self.c)
            self.arrived(slot)
            self.push(slot, self.sibling())
            use(slot)

    def fourth(self, use):
        for b in (self.b, 1 - self.b):
            for i in [0, 1, self.lines - 1] + list(range(2, self.lines - 1)):
                slot = self.slot(self.line(i), b, 1 - self.c)
                self.arrived(slot)
                use(slot)

    def finish(self):
        for copy in self.started:
            copy.wait_send()


def visible(meta, steps, rows, blocks):
    lane = lax.broadcasted_iota(jnp.int32, (rows, rows), 1)
    eye = (lane == lax.broadcasted_iota(jnp.int32, (rows, rows), 0)).astype(jnp.float32)
    picks = [(meta[:, t : t + 1] == lane.astype(jnp.float32)).astype(jnp.float32) for t in range(steps)]
    token = lax.broadcasted_iota(jnp.int32, (rows, blocks * BLOCK), 1)
    block = (token // BLOCK).astype(jnp.float32)
    offset = (token % BLOCK).astype(jnp.float32)
    place = lax.broadcasted_iota(jnp.int32, (rows, steps * rows), 1)
    own = lax.broadcasted_iota(jnp.int32, (rows, steps * rows), 0)
    cached, fresh, positions = [], [], []
    for step in range(steps):
        lineage = eye
        total = (place == own + step * rows).astype(jnp.float32)
        for earlier in range(step - 1, -1, -1):
            lineage = dot(lineage.astype(jnp.bfloat16), picks[earlier + 1].astype(jnp.bfloat16))
            spread = (place == own + earlier * rows).astype(jnp.bfloat16)
            total = total + dot(lineage.astype(jnp.bfloat16), spread)
        root = dot(lineage.astype(jnp.bfloat16), picks[0].astype(jnp.bfloat16))
        values = dot(root.astype(jnp.bfloat16), meta.astype(jnp.bfloat16))
        length = values[:, steps : steps + 1]
        count = jnp.zeros((rows, blocks * BLOCK), jnp.float32)
        for entry in range(2):
            named = values[:, steps + 1 + entry : steps + 2 + entry] == block
            inside = offset + float(entry * BLOCK) < length
            count = count + (named & inside).astype(jnp.float32)
        cached.append(count)
        fresh.append(total)
        positions.append(length + float(step))
    return jnp.concatenate(cached), jnp.concatenate(fresh), jnp.concatenate(positions)


def kernel(
    n, segments, steps,
    x_ref, gain_ref, meta_ref, freq_ref, wq_hbm, kv_hbm, wo_hbm, cache_hbm,
    out_ref,
    wq, kv, wo, cache, xbuf, nbuf, abuf, kvbuf, sel, inc, res,
    cached_ref, fresh_ref, cos_ref, sin_ref, total,
    load_sem, x_send, x_recv, k_send, k_recv, a_send, a_recv, hop_send, hop_recv,
):
    segment = lax.axis_index("segment")
    me = lax.axis_index("tensor")
    items, width = x_ref.shape
    rows = items // steps
    features = n * width
    blocks = cache.shape[0] // BLOCK
    lines = n // (COLUMNS * CORES)
    kv_columns = kv.shape[0] // 2
    channels = kv_columns // KV_HEADS
    heads = wq.shape[1] // HEAD_SIZE
    kv_head = me * heads // GROUP

    loads = [
        pltpu.make_async_copy(src, dst, load_sem.at[i])
        for i, (src, dst) in enumerate(((kv_hbm, kv), (wq_hbm, wq), (cache_hbm, cache), (wo_hbm, wo)))
    ]
    for load in loads:
        load.start()

    gx = Gather(xbuf, x_send, x_recv, me, lines)
    gk = Gather(kvbuf, k_send, k_recv, me, lines)
    ga = Gather(abuf, a_send, a_recv, me, lines)
    following = lax.rem(segment + 1, segments)
    before = lax.rem(segment + segments - 1, segments)

    barrier = pltpu.get_barrier_semaphore()
    peers = gx.peers()
    for peer in peers:
        pl.semaphore_signal(barrier, inc=1, device_id={"tensor": peer}, device_id_type=MESH)
    ends = [following] if segments == 2 else [following, before]
    for end in ends:
        pl.semaphore_signal(barrier, inc=1, device_id={"segment": end}, device_id_type=MESH)
    pl.semaphore_wait(barrier, len(peers) + len(ends))

    hop = pltpu.make_async_remote_copy(
        src_ref=res, dst_ref=inc, send_sem=hop_send, recv_sem=hop_recv,
        device_id={"segment": following}, device_id_type=MESH,
    )

    def prepare():
        cached, fresh, position = visible(meta_ref[...], steps, rows, blocks)
        cached_ref[...] = cached
        fresh_ref[...] = fresh
        angle = position * freq_ref[...]
        cos_ref[...] = jnp.cos(angle)
        half = lax.broadcasted_iota(jnp.int32, (items, HEAD_SIZE), 1) < HEAD_SIZE // 2
        sine = jnp.sin(angle)
        sin_ref[...] = jnp.where(half, -sine, sine)

        def fill(d, carry):
            line = lax.broadcasted_iota(jnp.int32, (2 * kv_columns, 2 * HEAD_SIZE), 0)
            column = lax.broadcasted_iota(jnp.int32, (2 * kv_columns, 2 * HEAD_SIZE), 1)
            inner = line % kv_columns
            goal = line // kv_columns * HEAD_SIZE + d * channels + inner // KV_HEADS
            hit = (inner % KV_HEADS == kv_head) & (column == goal)
            sel[d] = hit.astype(jnp.float32).astype(jnp.bfloat16)
            return carry

        lax.fori_loop(0, n, fill, 0)

    @pl.when(segment == 0)
    def _():
        xbuf[me] = x_ref[...]

    @pl.when(segment > 0)
    def _():
        prepare()
        hop.wait_recv()
        xbuf[me] = inc[...]

    def nothing(slot):
        pass

    total[...] = jnp.zeros_like(total)

    def squares(slot):
        chunk = xbuf[slot].astype(jnp.float32)
        total[...] += jnp.sum(chunk * chunk, axis=1, keepdims=True)

    gx.first(squares)

    @pl.when(segment == 0)
    def _():
        prepare()

    gx.second(squares)
    gx.third(squares)
    gx.fourth(squares)
    inverse = lax.rsqrt(total[...] * (1.0 / features) + NORM_EPS)

    loads[0].wait()

    def project_kv(s, acc):
        normed = (xbuf[s].astype(jnp.float32) * inverse * gain_ref[s]).astype(jnp.bfloat16)
        nbuf[s] = normed
        return acc + dot_nt(normed, kv[:, pl.ds(pl.multiple_of(s * width, width), width)])

    kv_own = lax.fori_loop(0, n, project_kv, jnp.zeros((items, 2 * kv_columns), jnp.float32))
    kvbuf[me] = kv_own.astype(jnp.bfloat16)
    gk.first(nothing)
    loads[1].wait()

    def project_q(s, acc):
        return acc + dot(nbuf[s], wq[pl.ds(pl.multiple_of(s * width, width), width), :])

    query = jnp.zeros((items, wq.shape[1]), jnp.float32)
    query = lax.fori_loop(0, n // 2, project_q, query)
    gk.second(nothing)
    query = lax.fori_loop(n // 2, n, project_q, query)
    gk.third(nothing)

    cos, sin = cos_ref[...], sin_ref[...]

    def rotated(values):
        return (values * cos + pltpu.roll(values, HEAD_SIZE // 2, 1) * sin).astype(jnp.bfloat16)

    turned = jnp.concatenate([rotated(query[:, h * HEAD_SIZE : (h + 1) * HEAD_SIZE]) for h in range(heads)])
    loads[2].wait()
    scale = HEAD_SIZE**-0.5
    keys = cache[:, :HEAD_SIZE]
    cached = jnp.concatenate([cached_ref[...]] * heads)
    fresh = jnp.concatenate([fresh_ref[...]] * heads)
    old_scores = jnp.where(cached > 0.0, dot_nt(turned, keys) * scale, MASK_FLOOR)
    gk.fourth(nothing)

    def collect(d, acc):
        return acc + dot(kvbuf[d], sel[d])

    entry = lax.fori_loop(0, n, collect, jnp.zeros((items, 2 * HEAD_SIZE), jnp.float32))
    new_key = rotated(entry[:, :HEAD_SIZE])
    new_value = entry[:, HEAD_SIZE:].astype(jnp.bfloat16)
    new_scores = jnp.where(fresh > 0.0, dot_nt(turned, new_key) * scale, MASK_FLOOR)
    highest = jnp.maximum(
        jnp.max(old_scores, axis=1, keepdims=True), jnp.max(new_scores, axis=1, keepdims=True)
    )
    old_exp = jnp.exp(old_scores - highest)
    new_exp = jnp.exp(new_scores - highest)
    denominator = jnp.sum(old_exp * cached, axis=1, keepdims=True) + jnp.sum(
        new_exp * fresh, axis=1, keepdims=True
    )
    old_probs = ((old_exp / denominator).astype(jnp.bfloat16).astype(jnp.float32) * cached).astype(jnp.bfloat16)
    new_probs = ((new_exp / denominator).astype(jnp.bfloat16).astype(jnp.float32) * fresh).astype(jnp.bfloat16)
    mixture = dot(old_probs, cache[:, HEAD_SIZE:]) + dot(new_probs, new_value)
    mixture = mixture.astype(jnp.bfloat16)
    for h in range(heads):
        abuf[me, :, h * HEAD_SIZE : (h + 1) * HEAD_SIZE] = mixture[h * items : (h + 1) * items]

    loads[3].wait()
    update = [xbuf[me].astype(jnp.float32), jnp.zeros((items, wo.shape[1]), jnp.float32)]

    def project_out(slot):
        update[1] = update[1] + dot(abuf[slot], wo[pl.ds(pl.multiple_of(slot * width, width), width), :])

    ga.first(project_out)
    ga.second(project_out)
    ga.third(project_out)
    ga.fourth(project_out)
    res[...] = (update[0] + update[1]).astype(jnp.bfloat16)
    hop.start()
    gx.finish()
    gk.finish()
    ga.finish()
    hop.wait_send()

    @pl.when(segment == 0)
    def _():
        hop.wait_recv()

    out_ref[...] = inc[...]


def per_device(
    n, segments, step_inputs, norm_gain, query_weight, kv_weight, out_weight, kv_cache, block_table, prefix_len, parents
):
    steps, rows, width = step_inputs.shape
    items = steps * rows
    kv_columns = kv_weight.shape[3]
    features = kv_weight.shape[1]
    blocks = kv_cache.shape[2]
    heads = query_weight.shape[2] // HEAD_SIZE
    start = jnp.arange(rows, dtype=jnp.int32)[:, None] // BEAMS * BEAMS
    meta = jnp.concatenate(
        [parents.T + start, prefix_len[:, None], block_table], axis=1
    ).astype(jnp.float32)
    exponent = jnp.arange(HEAD_SIZE // 2, dtype=jnp.float32) * (2.0 / HEAD_SIZE)
    frequency = jnp.power(jnp.float32(ROPE_BASE), -exponent)
    frequency = jnp.concatenate([frequency, frequency])[None, :]
    lines = n // (COLUMNS * CORES)
    sends = 4 * lines - 1
    bf16, f32 = jnp.bfloat16, jnp.float32
    vmem = pl.BlockSpec(memory_space=pltpu.VMEM)
    hbm = pl.BlockSpec(memory_space=pltpu.HBM)
    dma = pltpu.SemaphoreType.DMA
    received = pl.pallas_call(
        functools.partial(kernel, n, segments, steps),
        out_shape=jax.ShapeDtypeStruct((items, width), bf16),
        in_specs=[vmem] * 4 + [hbm] * 4,
        out_specs=vmem,
        scratch_shapes=[
            pltpu.VMEM((features, query_weight.shape[2]), bf16),
            pltpu.VMEM((2 * kv_columns, features), bf16),
            pltpu.VMEM((out_weight.shape[1], width), bf16),
            pltpu.VMEM((blocks * BLOCK, 2 * HEAD_SIZE), bf16),
            pltpu.VMEM((n, items, width), bf16),
            pltpu.VMEM((n, items, width), bf16),
            pltpu.VMEM((n, items, heads * HEAD_SIZE), bf16),
            pltpu.VMEM((n, items, 2 * kv_columns), bf16),
            pltpu.VMEM((n, 2 * kv_columns, 2 * HEAD_SIZE), bf16),
            pltpu.VMEM((items, width), bf16),
            pltpu.VMEM((items, width), bf16),
            pltpu.VMEM((items, blocks * BLOCK), f32),
            pltpu.VMEM((items, items), f32),
            pltpu.VMEM((items, HEAD_SIZE), f32),
            pltpu.VMEM((items, HEAD_SIZE), f32),
            pltpu.VMEM((items, 1), f32),
            dma((4,)),
            dma((sends,)), dma((n,)),
            dma((sends,)), dma((n,)),
            dma((sends,)), dma((n,)),
            dma, dma,
        ],
        compiler_params=pltpu.CompilerParams(
            collective_id=0, has_side_effects=True, vmem_limit_bytes=52 * 2**20
        ),
    )(
        step_inputs.reshape(items, width),
        norm_gain.reshape(n, 1, width),
        meta,
        frequency,
        query_weight[0],
        kv_weight[0].transpose(1, 2, 0).reshape(2 * kv_columns, features),
        out_weight[0],
        kv_cache.reshape(blocks * BLOCK, 2 * HEAD_SIZE),
    )
    return received.reshape(1, steps, rows, width)


def solution(mesh):
    return jax.shard_map(
        functools.partial(per_device, mesh.shape["tensor"], mesh.shape["segment"]),
        mesh=mesh,
        in_specs=(
            P(None, None, "tensor"),
            P("segment", None),
            P("segment", None, "tensor"),
            P("segment", None, None, "tensor"),
            P("segment", None, "tensor"),
            P("segment", "tensor", None, None, None),
            P(),
            P(),
            P(),
        ),
        out_specs=P("segment", None, None, "tensor"),
        check_vma=False,
    )
```

time: 344 us -> 88.7 us (0.26)
  blocking collectives: 233 us -> 0 us
  Pallas kernels: 0 us -> 82.8 us
  matrix products: 54.9 us -> 0 us
  local copies, waits for them, and re-layouts: 27.8 us -> 5.36 us
  other arithmetic: 8.74 us -> 0.25 us
  waiting for transfers between devices: 6.44 us -> 0 us
  starting transfers between devices: 6.03 us -> 0 us
  loops' own time: 5.8 us -> 0 us
    all_gather x12 -> x0, blocking collectives: 233 us -> none  [the longest x4 79.6 us: advance(): full_rows = lax.all_gather(current, 'tensor', axis=1, tiled=True)]
    pallas_call x0 -> x1, Pallas kernels: none -> 82.8 us  [per_device(): pl.pallas_call(functools.partial(kernel, n, segments, steps), out_shape=j...]
    dot_general x28 -> x0, matrix products: 54.9 us -> none  [the longest x4 18.5 us: advance(): jnp.dot(normed, query_local, preferred_element_type=jnp.float32)]
    gather x30 -> x0, local copies, waits for them, and re-layouts: 20.8 us -> none  [the longest x4 8.11 us: advance(): blocks = cache_local[table_rows].reshape(BEAMS, 2 * BLOCK, 2 * HEAD_SIZE)]
    ppermute x4 -> x0, waiting for transfers between devices: 6.44 us -> none  [shifted(): return lax.ppermute(block, axis, route)]
    ppermute x4 -> x0, starting transfers between devices: 6.03 us -> none  [shifted(): return lax.ppermute(block, axis, route)]
    another operation x1 -> x0, loops' own time: 5.8 us -> none  [per_device(): sweep_loop_state, unused = lax.scan(scan_step, sweep_loop_state, ticks)]
    unnamed x12 -> x9, local copies, waits for them, and re-layouts: 0.63 us -> 4.62 us
  transfers between devices with their start and end apart: 4 -> 0, of which waited for: 4 -> 0; matrix products, arithmetic and copies ran while one was open for 0% -> 0% of each run, Pallas kernels for 0% -> 0%
where the time goes in v1:
time: 88.7 us; the launch traced here: 88.4 us
  Pallas kernels  82.8 us (93%)
  local copies, waits for them, and re-layouts  5.36 us (6%)
    pallas_call x1, Pallas kernels, per_device(): pl.pallas_call(functools.partial(kernel, n, segments, steps), out_shape=j...  82.8 us
    unnamed x9, local copies, waits for them, and re-layouts  4.62 us

profile of v1, /device:TPU:0, one launch (start us, length us, event | category | flops | bytes accessed | tf_op | source)
XLA Modules:
  0.0 88.4 jit_solution(8806090403469318726)
XLA Ops:
  0.0 0.1 maximum_bitcast_fusion.freq_ref
  0.1 0.8 copy.16
  0.9 0.7 copy.15
  1.6 0.8 copy.13
  2.3 0.1 add_bitcast_fusion
  2.4 0.1 add_convert_fusion.meta_ref
  2.5 0.0 copy-start
  2.5 0.9 %copy-done = bf16[1,1,3,128,256]{4,3,2,1,0:T(8,128)(2,1)S(1)} copy-done((bf16[1,1,3,128,256]{4,3,2,1,0:T(8,128)(2,1)S(1)}, bf16[1,1,3,128,256]{4,3,2,1,0:T(8,128)(2,1)}, u32[]{:S(2)}) %copy-start) | copy-done | bytes 196632
  3.4 0.0 copy-start.1
  3.4 0.8 copy-done.1
  4.2 0.0 copy-start.2
  4.2 0.8 copy-done.2
  5.0 82.8 %shard_map.91 = bf16[48,512]{1,0:T(8,128)(2,1)S(1)} custom-call(bf16[48,512]{1,0:T(8,128)(2,1)S(1)} %bitcast.18, f32[16,1,512]{2,1,0:T(1,128)S(1)} %bitcast.19, f32[16,6]{1,0:T(8,128)S(1)} %add_convert_fusion.meta_ref, f32[1,128]{1,0:T(1,128)S(1)} %maximum_bitcast_fusion.freq_ref, bf16[8192,512]{1,0:T(8,128)(2,1)} %bitcast.20, bf16[128,8192]{1,0:T(8,128)(2,1)} %bitcast.22, ...), custom_call_target="tpu_custom_call" | custom-call | tf_op jit(solution)/shard_map/pallas_call | solution.py:342
  87.8 0.6 copy.18
  (2 shorter events, 0.0 us)
Async XLA Ops:
  2.5 0.9 %copy-start = (bf16[1,1,3,128,256]{4,3,2,1,0:T(8,128)(2,1)S(1)}, bf16[1,1,3,128,256]{4,3,2,1,0:T(8,128)(2,1)}, u32[]{:S(2)}) copy-start(bf16[1,1,3,128,256]{4,3,2,1,0:T(8,128)(2,1)} %param.14) | copy-start | bytes 589828
  3.4 0.8 copy-start.1
  4.2 0.8 copy-start.2

commit v2 on v1

--- a/solution.py
+++ b/solution.py
@@ -107,13 +107,18 @@
             copy.wait_send()
 
 
-def visible(meta, steps, rows, blocks):
+def log2(size):
+    return size.bit_length() - 1
+
+
+def visible(listed, steps, rows, blocks):
     lane = lax.broadcasted_iota(jnp.int32, (rows, rows), 1)
     eye = (lane == lax.broadcasted_iota(jnp.int32, (rows, rows), 0)).astype(jnp.float32)
+    meta = dot_nt(eye.astype(jnp.bfloat16), listed.astype(jnp.bfloat16))
     picks = [(meta[:, t : t + 1] == lane.astype(jnp.float32)).astype(jnp.float32) for t in range(steps)]
     token = lax.broadcasted_iota(jnp.int32, (rows, blocks * BLOCK), 1)
-    block = (token // BLOCK).astype(jnp.float32)
-    offset = (token % BLOCK).astype(jnp.float32)
+    block = (token >> log2(BLOCK)).astype(jnp.float32)
+    offset = (token & (BLOCK - 1)).astype(jnp.float32)
     place = lax.broadcasted_iota(jnp.int32, (rows, steps * rows), 1)
     own = lax.broadcasted_iota(jnp.int32, (rows, steps * rows), 0)
     cached, fresh, positions = [], [], []
@@ -140,15 +145,15 @@
 
 def kernel(
     n, segments, steps,
-    x_ref, gain_ref, meta_ref, freq_ref, wq_hbm, kv_hbm, wo_hbm, cache_hbm,
+    meta_ref, freq_ref, x_hbm, gain_hbm, wq_hbm, kv_hbm, wo_hbm, cache_hbm,
     out_ref,
-    wq, kv, wo, cache, xbuf, nbuf, abuf, kvbuf, sel, inc, res,
+    gain_ref, wq, kv, wo, cache, xbuf, nbuf, abuf, kvbuf, sel, inc, res,
     cached_ref, fresh_ref, cos_ref, sin_ref, total,
     load_sem, x_send, x_recv, k_send, k_recv, a_send, a_recv, hop_send, hop_recv,
 ):
     segment = lax.axis_index("segment")
     me = lax.axis_index("tensor")
-    items, width = x_ref.shape
+    items, width = x_hbm.shape
     rows = items // steps
     features = n * width
     blocks = cache.shape[0] // BLOCK
@@ -160,7 +165,12 @@
 
     loads = [
         pltpu.make_async_copy(src, dst, load_sem.at[i])
-        for i, (src, dst) in enumerate(((kv_hbm, kv), (wq_hbm, wq), (cache_hbm, cache), (wo_hbm, wo)))
+        for i, (src, dst) in enumerate(
+            (
+                (x_hbm, xbuf.at[me]), (gain_hbm, gain_ref), (kv_hbm, kv),
+                (wq_hbm, wq), (cache_hbm, cache), (wo_hbm, wo),
+            )
+        )
     ]
     for load in loads:
         load.start()
@@ -185,36 +195,51 @@
         device_id={"segment": following}, device_id_type=MESH,
     )
 
-    def prepare():
+    def prepare_masks():
         cached, fresh, position = visible(meta_ref[...], steps, rows, blocks)
         cached_ref[...] = cached
         fresh_ref[...] = fresh
-        angle = position * freq_ref[...]
+        cos_ref[...] = jnp.broadcast_to(position, cos_ref.shape)
+
+    def prepare_turns():
+        angle = cos_ref[...] * freq_ref[...]
         cos_ref[...] = jnp.cos(angle)
         half = lax.broadcasted_iota(jnp.int32, (items, HEAD_SIZE), 1) < HEAD_SIZE // 2
         sine = jnp.sin(angle)
         sin_ref[...] = jnp.where(half, -sine, sine)
 
+    def prepare_picks():
+        shape = (2 * kv_columns, 2 * HEAD_SIZE)
+        line = lax.broadcasted_iota(jnp.int32, shape, 0)
+        inner = line & (kv_columns - 1)
+        goal = (line >> log2(kv_columns)) * HEAD_SIZE + (inner >> log2(KV_HEADS))
+        goal = jnp.where((inner & (KV_HEADS - 1)) == kv_head, goal, -2 * HEAD_SIZE)
+        ahead = lax.broadcasted_iota(jnp.int32, shape, 1) - goal
+
         def fill(d, carry):
-            line = lax.broadcasted_iota(jnp.int32, (2 * kv_columns, 2 * HEAD_SIZE), 0)
-            column = lax.broadcasted_iota(jnp.int32, (2 * kv_columns, 2 * HEAD_SIZE), 1)
-            inner = line % kv_columns
-            goal = line // kv_columns * HEAD_SIZE + d * channels + inner // KV_HEADS
-            hit = (inner % KV_HEADS == kv_head) & (column == goal)
-            sel[d] = hit.astype(jnp.float32).astype(jnp.bfloat16)
+            sel[d] = (ahead == d * channels).astype(jnp.float32).astype(jnp.bfloat16)
             return carry
 
         lax.fori_loop(0, n, fill, 0)
+
+    def first_segment(part):
+        @pl.when(segment == 0)
+        def _():
+            part()
 
     @pl.when(segment == 0)
     def _():
-        xbuf[me] = x_ref[...]
+        loads[0].wait()
 
     @pl.when(segment > 0)
     def _():
-        prepare()
-        hop.wait_recv()
-        xbuf[me] = inc[...]
+        prepare_masks()
+        prepare_turns()
+        prepare_picks()
+        with jax.named_scope("wait_hop"):
+            loads[0].wait()
+            hop.wait_recv()
+            xbuf[me] = inc[...]
 
     def nothing(slot):
         pass
@@ -225,37 +250,41 @@
         chunk = xbuf[slot].astype(jnp.float32)
         total[...] += jnp.sum(chunk * chunk, axis=1, keepdims=True)
 
-    gx.first(squares)
-
-    @pl.when(segment == 0)
-    def _():
-        prepare()
-
-    gx.second(squares)
-    gx.third(squares)
-    gx.fourth(squares)
+    with jax.named_scope("gather_rows"):
+        gx.first(squares)
+        first_segment(prepare_masks)
+        gx.second(squares)
+        first_segment(prepare_turns)
+        gx.third(squares)
+        first_segment(prepare_picks)
+        gx.fourth(squares)
     inverse = lax.rsqrt(total[...] * (1.0 / features) + NORM_EPS)
 
-    loads[0].wait()
-
-    def project_kv(s, acc):
-        normed = (xbuf[s].astype(jnp.float32) * inverse * gain_ref[s]).astype(jnp.bfloat16)
-        nbuf[s] = normed
-        return acc + dot_nt(normed, kv[:, pl.ds(pl.multiple_of(s * width, width), width)])
-
-    kv_own = lax.fori_loop(0, n, project_kv, jnp.zeros((items, 2 * kv_columns), jnp.float32))
-    kvbuf[me] = kv_own.astype(jnp.bfloat16)
-    gk.first(nothing)
-    loads[1].wait()
-
-    def project_q(s, acc):
-        return acc + dot(nbuf[s], wq[pl.ds(pl.multiple_of(s * width, width), width), :])
-
-    query = jnp.zeros((items, wq.shape[1]), jnp.float32)
-    query = lax.fori_loop(0, n // 2, project_q, query)
-    gk.second(nothing)
-    query = lax.fori_loop(n // 2, n, project_q, query)
-    gk.third(nothing)
+    with jax.named_scope("normalize"):
+        loads[1].wait()
+        for s in range(n):
+            normed = xbuf[s].astype(jnp.float32) * inverse * gain_ref[:, s * width : (s + 1) * width]
+            nbuf[:, s * width : (s + 1) * width] = normed.astype(jnp.bfloat16)
+
+    part = features // 4
+
+    def project_q(i):
+        return dot(nbuf[:, i * part : (i + 1) * part], wq[i * part : (i + 1) * part, :])
+
+    with jax.named_scope("project_kv"):
+        loads[2].wait()
+        kv_own = dot_nt(nbuf[:, :part], kv[:, :part])
+        for i in range(1, 4):
+            kv_own = kv_own + dot_nt(nbuf[:, i * part : (i + 1) * part], kv[:, i * part : (i + 1) * part])
+        kvbuf[me] = kv_own.astype(jnp.bfloat16)
+        gk.first(nothing)
+    with jax.named_scope("project_query"):
+        loads[3].wait()
+        query = project_q(0) + project_q(1)
+        gk.second(nothing)
+        query = query + project_q(2)
+        gk.third(nothing)
+        query = query + project_q(3)
 
     cos, sin = cos_ref[...], sin_ref[...]
 
@@ -263,13 +292,14 @@
         return (values * cos + pltpu.roll(values, HEAD_SIZE // 2, 1) * sin).astype(jnp.bfloat16)
 
     turned = jnp.concatenate([rotated(query[:, h * HEAD_SIZE : (h + 1) * HEAD_SIZE]) for h in range(heads)])
-    loads[2].wait()
+    loads[4].wait()
     scale = HEAD_SIZE**-0.5
     keys = cache[:, :HEAD_SIZE]
     cached = jnp.concatenate([cached_ref[...]] * heads)
     fresh = jnp.concatenate([fresh_ref[...]] * heads)
     old_scores = jnp.where(cached > 0.0, dot_nt(turned, keys) * scale, MASK_FLOOR)
-    gk.fourth(nothing)
+    with jax.named_scope("wait_kv"):
+        gk.fourth(nothing)
 
     def collect(d, acc):
         return acc + dot(kvbuf[d], sel[d])
@@ -293,16 +323,18 @@
     for h in range(heads):
         abuf[me, :, h * HEAD_SIZE : (h + 1) * HEAD_SIZE] = mixture[h * items : (h + 1) * items]
 
-    loads[3].wait()
+    loads[5].wait()
     update = [xbuf[me].astype(jnp.float32), jnp.zeros((items, wo.shape[1]), jnp.float32)]
 
     def project_out(slot):
         update[1] = update[1] + dot(abuf[slot], wo[pl.ds(pl.multiple_of(slot * width, width), width), :])
 
-    ga.first(project_out)
-    ga.second(project_out)
-    ga.third(project_out)
-    ga.fourth(project_out)
+    with jax.named_scope("gather_attended"):
+        ga.first(project_out)
+        ga.second(project_out)
+        ga.third(project_out)
+    with jax.named_scope("last_attended"):
+        ga.fourth(project_out)
     res[...] = (update[0] + update[1]).astype(jnp.bfloat16)
     hop.start()
     gx.finish()
@@ -326,9 +358,9 @@
     features = kv_weight.shape[1]
     blocks = kv_cache.shape[2]
     heads = query_weight.shape[2] // HEAD_SIZE
-    start = jnp.arange(rows, dtype=jnp.int32)[:, None] // BEAMS * BEAMS
+    start = jnp.arange(rows, dtype=jnp.int32)[None, :] // BEAMS * BEAMS
     meta = jnp.concatenate(
-        [parents.T + start, prefix_len[:, None], block_table], axis=1
+        [parents + start, prefix_len[None, :], block_table.T], axis=0
     ).astype(jnp.float32)
     exponent = jnp.arange(HEAD_SIZE // 2, dtype=jnp.float32) * (2.0 / HEAD_SIZE)
     frequency = jnp.power(jnp.float32(ROPE_BASE), -exponent)
@@ -342,15 +374,16 @@
     received = pl.pallas_call(
         functools.partial(kernel, n, segments, steps),
         out_shape=jax.ShapeDtypeStruct((items, width), bf16),
-        in_specs=[vmem] * 4 + [hbm] * 4,
+        in_specs=[vmem] * 2 + [hbm] * 6,
         out_specs=vmem,
         scratch_shapes=[
+            pltpu.VMEM((1, features), f32),
             pltpu.VMEM((features, query_weight.shape[2]), bf16),
             pltpu.VMEM((2 * kv_columns, features), bf16),
             pltpu.VMEM((out_weight.shape[1], width), bf16),
             pltpu.VMEM((blocks * BLOCK, 2 * HEAD_SIZE), bf16),
             pltpu.VMEM((n, items, width), bf16),
-            pltpu.VMEM((n, items, width), bf16),
+            pltpu.VMEM((items, features), bf16),
             pltpu.VMEM((n, items, heads * HEAD_SIZE), bf16),
             pltpu.VMEM((n, items, 2 * kv_columns), bf16),
             pltpu.VMEM((n, 2 * kv_columns, 2 * HEAD_SIZE), bf16),
@@ -361,20 +394,20 @@
             pltpu.VMEM((items, HEAD_SIZE), f32),
             pltpu.VMEM((items, HEAD_SIZE), f32),
             pltpu.VMEM((items, 1), f32),
-            dma((4,)),
+            dma((6,)),
             dma((sends,)), dma((n,)),
             dma((sends,)), dma((n,)),
             dma((sends,)), dma((n,)),
             dma, dma,
         ],
         compiler_params=pltpu.CompilerParams(
-            collective_id=0, has_side_effects=True, vmem_limit_bytes=52 * 2**20
+            collective_id=0, has_side_effects=True, vmem_limit_bytes=127 * 2**19
         ),
     )(
-        step_inputs.reshape(items, width),
-        norm_gain.reshape(n, 1, width),
         meta,
         frequency,
+        step_inputs.reshape(items, width),
+        norm_gain,
         query_weight[0],
         kv_weight[0].transpose(1, 2, 0).reshape(2 * kv_columns, features),
         out_weight[0],

time: 88.7 us -> 84.4 us (0.952)
  local copies, waits for them, and re-layouts: 5.36 us -> 1.42 us
  Pallas kernels: 82.8 us -> 80.1 us
  other arithmetic: 0.25 us -> 2.64 us
    unnamed x9 -> x1, local copies, waits for them, and re-layouts: 4.62 us -> 1.42 us
    pallas_call x1, Pallas kernels: 82.8 us -> 80.1 us  [per_device(): pl.pallas_call(functools.partial(kernel, n, segments, steps), out_shape=j...]
    convert_element_type x1, other arithmetic: 0.08 us -> 1.28 us  [per_device(): meta = jnp.concatenate([parents + start, prefix_len[None, :], block_table...]
where the time goes in v2:
time: 84.4 us; the launch traced here: 84.2 us
  Pallas kernels  80.1 us (95%)
  other arithmetic  2.64 us (3%)
  local copies, waits for them, and re-layouts  1.42 us (2%)
    pallas_call x1, Pallas kernels, per_device(): pl.pallas_call(functools.partial(kernel, n, segments, steps), out_shape=j...  80.1 us

profile of v2, /device:TPU:0, one launch (start us, length us, event | category | flops | bytes accessed | tf_op | source)
XLA Modules:
  0.0 84.2 jit_solution(3571507259618016518)
XLA Ops:
  0.0 0.7 maximum_bitcast_fusion.freq_ref
  0.7 0.7 broadcast_add_fusion
  1.4 1.3 %add_convert_fusion.meta_ref = f32[6,16]{1,0:T(8,128)} fusion(s32[2,16]{1,0:T(2,128)} %bitcast.20, s32[1,16]{1,0:T(1,128)} %bitcast.21, s32[3,16]{1,0:T(4,128)S(1)} %broadcast_add_fusion), kind=kLoop, calls=%fused_computation | loop fusion | flops 288 | bytes 768 | tf_op jit(solution)/shard_map/convert_element_type | solution.py:364
  2.6 80.1 %shard_map.91 = bf16[48,512]{1,0:T(8,128)(2,1)} custom-call(f32[6,16]{1,0:T(8,128)} %add_convert_fusion.meta_ref, f32[1,128]{1,0:T(1,128)} %maximum_bitcast_fusion.freq_ref, bf16[48,512]{1,0:T(8,128)(2,1)} %bitcast.19, f32[1,8192]{1,0:T(1,128)} %gain_hbm.1, bf16[8192,512]{1,0:T(8,128)(2,1)} %bitcast.14, bf16[128,8192]{1,0:T(8,128)(2,1)} %bitcast.16, ...), custom_call_target="tpu_custom_call" | custom-call | tf_op jit(solution)/shard_map/pallas_call | solution.py:374
  82.8 1.4 %copy.11 = bf16[1,3,16,512]{3,2,1,0:T(8,128)(2,1)} copy(bf16[1,3,16,512]{3,2,1,0:T(8,128)(2,1)} %bitcast.18) | data formatting | bytes 98304
  (2 shorter events, 0.0 us)

commit v3 on v2

--- a/solution.py
+++ b/solution.py
@@ -1,4 +1,5 @@
 import functools
+import math
 
 import jax
 import jax.numpy as jnp
@@ -145,9 +146,9 @@
 
 def kernel(
     n, segments, steps,
-    meta_ref, freq_ref, x_hbm, gain_hbm, wq_hbm, kv_hbm, wo_hbm, cache_hbm,
+    x_hbm, gain_hbm, wq_hbm, kv_hbm, wo_hbm, cache_hbm, parents_hbm, length_hbm, table_hbm,
     out_ref,
-    gain_ref, wq, kv, wo, cache, xbuf, nbuf, abuf, kvbuf, sel, inc, res,
+    parents_ref, length_ref, table_ref, listed_ref, gain_ref, wq, kv, wo, cache, xbuf, nbuf, abuf, kvbuf, sel, inc, res,
     cached_ref, fresh_ref, cos_ref, sin_ref, total,
     load_sem, x_send, x_recv, k_send, k_recv, a_send, a_recv, hop_send, hop_recv,
 ):
@@ -169,6 +170,7 @@
             (
                 (x_hbm, xbuf.at[me]), (gain_hbm, gain_ref), (kv_hbm, kv),
                 (wq_hbm, wq), (cache_hbm, cache), (wo_hbm, wo),
+                (parents_hbm, parents_ref), (length_hbm, length_ref), (table_hbm, table_ref),
             )
         )
     ]
@@ -196,13 +198,21 @@
     )
 
     def prepare_masks():
-        cached, fresh, position = visible(meta_ref[...], steps, rows, blocks)
+        for load in loads[6:]:
+            load.wait()
+        base = (lax.broadcasted_iota(jnp.int32, (steps, rows), 1) >> log2(BEAMS)) << log2(BEAMS)
+        listed_ref[0:steps] = (parents_ref[...] + base).astype(jnp.float32)
+        listed_ref[steps : steps + 1] = length_ref[...].astype(jnp.float32)
+        listed_ref[steps + 1 : steps + 3] = table_ref[...].astype(jnp.float32)
+        cached, fresh, position = visible(listed_ref[...], steps, rows, blocks)
         cached_ref[...] = cached
         fresh_ref[...] = fresh
         cos_ref[...] = jnp.broadcast_to(position, cos_ref.shape)
 
     def prepare_turns():
-        angle = cos_ref[...] * freq_ref[...]
+        index = lax.broadcasted_iota(jnp.int32, (items, HEAD_SIZE), 1) & (HEAD_SIZE // 2 - 1)
+        frequency = jnp.exp(index.astype(jnp.float32) * (-2.0 / HEAD_SIZE * math.log(ROPE_BASE)))
+        angle = cos_ref[...] * frequency
         cos_ref[...] = jnp.cos(angle)
         half = lax.broadcasted_iota(jnp.int32, (items, HEAD_SIZE), 1) < HEAD_SIZE // 2
         sine = jnp.sin(angle)
@@ -331,8 +341,11 @@
 
     with jax.named_scope("gather_attended"):
         ga.first(project_out)
-        ga.second(project_out)
-        ga.third(project_out)
+        waiting = []
+        ga.second(waiting.append)
+        ga.third(waiting.append)
+        for slot in waiting:
+            project_out(slot)
     with jax.named_scope("last_attended"):
         ga.fourth(project_out)
     res[...] = (update[0] + update[1]).astype(jnp.bfloat16)
@@ -358,13 +371,6 @@
     features = kv_weight.shape[1]
     blocks = kv_cache.shape[2]
     heads = query_weight.shape[2] // HEAD_SIZE
-    start = jnp.arange(rows, dtype=jnp.int32)[None, :] // BEAMS * BEAMS
-    meta = jnp.concatenate(
-        [parents + start, prefix_len[None, :], block_table.T], axis=0
-    ).astype(jnp.float32)
-    exponent = jnp.arange(HEAD_SIZE // 2, dtype=jnp.float32) * (2.0 / HEAD_SIZE)
-    frequency = jnp.power(jnp.float32(ROPE_BASE), -exponent)
-    frequency = jnp.concatenate([frequency, frequency])[None, :]
     lines = n // (COLUMNS * CORES)
     sends = 4 * lines - 1
     bf16, f32 = jnp.bfloat16, jnp.float32
@@ -374,9 +380,13 @@
     received = pl.pallas_call(
         functools.partial(kernel, n, segments, steps),
         out_shape=jax.ShapeDtypeStruct((items, width), bf16),
-        in_specs=[vmem] * 2 + [hbm] * 6,
+        in_specs=[hbm] * 9,
         out_specs=vmem,
         scratch_shapes=[
+            pltpu.VMEM((steps, rows), jnp.int32),
+            pltpu.VMEM((1, rows), jnp.int32),
+            pltpu.VMEM((2, rows), jnp.int32),
+            pltpu.VMEM((steps + 3, rows), f32),
             pltpu.VMEM((1, features), f32),
             pltpu.VMEM((features, query_weight.shape[2]), bf16),
             pltpu.VMEM((2 * kv_columns, features), bf16),
@@ -394,7 +404,7 @@
             pltpu.VMEM((items, HEAD_SIZE), f32),
             pltpu.VMEM((items, HEAD_SIZE), f32),
             pltpu.VMEM((items, 1), f32),
-            dma((6,)),
+            dma((9,)),
             dma((sends,)), dma((n,)),
             dma((sends,)), dma((n,)),
             dma((sends,)), dma((n,)),
@@ -404,14 +414,15 @@
             collective_id=0, has_side_effects=True, vmem_limit_bytes=127 * 2**19
         ),
     )(
-        meta,
-        frequency,
         step_inputs.reshape(items, width),
         norm_gain,
         query_weight[0],
         kv_weight[0].transpose(1, 2, 0).reshape(2 * kv_columns, features),
         out_weight[0],
         kv_cache.reshape(blocks * BLOCK, 2 * HEAD_SIZE),
+        parents,
+        prefix_len[None, :],
+        block_table.T,
     )
     return received.reshape(1, steps, rows, width)
 

time: 84.4 us -> 83.4 us (0.988)
  other arithmetic: 2.64 us -> 0 us
  Pallas kernels: 80.1 us -> 81.8 us
    pallas_call x1, Pallas kernels: 80.1 us -> 81.8 us  [per_device(): pl.pallas_call(functools.partial(kernel, n, segments, steps), out_shape=j...]
    convert_element_type x1 -> x0, other arithmetic: 1.28 us -> none  [per_device(): meta = jnp.concatenate([parents + start, prefix_len[None, :], block_table...]
where the time goes in v3:
time: 83.4 us; the launch traced here: 83.3 us
  Pallas kernels  81.8 us (98%)
  local copies, waits for them, and re-layouts  1.42 us (2%)
    pallas_call x1, Pallas kernels, per_device(): pl.pallas_call(functools.partial(kernel, n, segments, steps), out_shape=j...  81.8 us

profile of v3, /device:TPU:0, one launch (start us, length us, event | category | flops | bytes accessed | tf_op | source)
XLA Modules:
  0.0 83.3 jit_solution(18279439265892498011)
XLA Ops:
  0.0 81.8 %shard_map.91 = bf16[48,512]{1,0:T(8,128)(2,1)} custom-call(bf16[48,512]{1,0:T(8,128)(2,1)} %bitcast.17, f32[1,8192]{1,0:T(1,128)} %gain_hbm.1, bf16[8192,512]{1,0:T(8,128)(2,1)} %bitcast.12, bf16[128,8192]{1,0:T(8,128)(2,1)} %bitcast.14, bf16[8192,512]{1,0:T(8,128)(2,1)} %bitcast.13, bf16[384,256]{1,0:T(8,128)(2,1)} %bitcast.15, s32[3,16]{1,0:T(4,128)} %parents_hbm.1, ...), custom_call_target="tpu_custom_call" | custom-call | tf_op jit(solution)/shard_map/pallas_call | solution.py:380
  81.9 1.4 %copy.11 = bf16[1,3,16,512]{3,2,1,0:T(8,128)(2,1)} copy(bf16[1,3,16,512]{3,2,1,0:T(8,128)(2,1)} %bitcast.16) | data formatting | bytes 98304

commit v4 on v3

--- a/solution.py
+++ b/solution.py
@@ -262,10 +262,13 @@
 
     with jax.named_scope("gather_rows"):
         gx.first(squares)
+        early = []
+        gx.second(early.append)
+        gx.third(early.append)
+        for slot in early:
+            squares(slot)
         first_segment(prepare_masks)
-        gx.second(squares)
         first_segment(prepare_turns)
-        gx.third(squares)
         first_segment(prepare_picks)
         gx.fourth(squares)
     inverse = lax.rsqrt(total[...] * (1.0 / features) + NORM_EPS)

time: 83.4 us -> 83.7 us (level)
  no operation moved by 1% of the time
where the time goes in v4:
time: 83.7 us; the launch traced here: 83.6 us
  Pallas kernels  82.1 us (98%)
  local copies, waits for them, and re-layouts  1.42 us (2%)
    pallas_call x1, Pallas kernels, per_device(): pl.pallas_call(functools.partial(kernel, n, segments, steps), out_shape=j...  82.1 us

profile of v4, /device:TPU:0, one launch (start us, length us, event | category | flops | bytes accessed | tf_op | source)
XLA Modules:
  0.0 83.6 jit_solution(7354566160598375212)
XLA Ops:
  0.0 82.1 %shard_map.91 = bf16[48,512]{1,0:T(8,128)(2,1)} custom-call(bf16[48,512]{1,0:T(8,128)(2,1)} %bitcast.17, f32[1,8192]{1,0:T(1,128)} %gain_hbm.1, bf16[8192,512]{1,0:T(8,128)(2,1)} %bitcast.12, bf16[128,8192]{1,0:T(8,128)(2,1)} %bitcast.14, bf16[8192,512]{1,0:T(8,128)(2,1)} %bitcast.13, bf16[384,256]{1,0:T(8,128)(2,1)} %bitcast.15, s32[3,16]{1,0:T(4,128)} %parents_hbm.1, ...), custom_call_target="tpu_custom_call" | custom-call | tf_op jit(solution)/shard_map/pallas_call | solution.py:383
  82.1 1.4 %copy.11 = bf16[1,3,16,512]{3,2,1,0:T(8,128)(2,1)} copy(bf16[1,3,16,512]{3,2,1,0:T(8,128)(2,1)} %bitcast.16) | data formatting | bytes 98304
